TPU v7x, 32 devices: a whole 2x2x4 slice. The times are simulated.
32 devices in a mesh: rep: 4 (over y, x), exp: 8 (over z, core).
Axes of the slice: x: 2, y: 2, z: 4, core: 2. Of those that a mesh axis runs over, the one named last changes fastest.
Arguments:
- tokens: bfloat16 [4096, 2048], P(('rep', 'exp')), may hold values from -6 to 6
- grad_out: bfloat16 [4096, 2048], P(('rep', 'exp')), may hold values from -6 to 6
- routes: int32 [4096, 2], P(('rep', 'exp')), may hold values from 0 to 7, all different within a row; in each aligned block of 128 rows (0 to 127, 128 to 255, ...) at most 64 rows name the same one
- gates: float32 [4096, 2], P(('rep', 'exp')), may hold values from 0.1 to 1
- w_gate: bfloat16 [8, 2048, 768], P('exp', 'rep'), may hold values from -0.125 to 0.125
- w_up: bfloat16 [8, 2048, 768], P('exp', 'rep'), may hold values from -0.125 to 0.125
- w_down: bfloat16 [8, 2048, 768], P('exp', 'rep'), may hold values from -0.125 to 0.125
Outputs:
- grad_gate: float32 [8, 2048, 768], P('exp', 'rep')
- grad_up: float32 [8, 2048, 768], P('exp', 'rep')
- grad_down: float32 [8, 2048, 768], P('exp', 'rep')
- grad_in: bfloat16 [4096, 2048], P(('rep', 'exp'))
Inputs may be any that keep to these rules, and one draw needn't show every extreme that they name: `routes`: each row names 2 different experts. Among the 128 rows of one device no expert is named more than 64 times, and in every draw some device names some expert exactly 64 times; every expert is named somewhere.
All inputs are finite; a program needn't handle non-finite values.
Results may differ from a plain program's by a relative error of at most 0.0065.
Values may be sent and summed in bfloat16 or wider, within the bound.
A program may use at most 128 MiB of HBM per device.

v0:
```python
import jax
import jax.numpy as jnp
from jax import lax
from jax.sharding import PartitionSpec as P


def contract_rows(left, right):
    return lax.dot_general(
        left, right, (((0,), (0,)), ((), ())), preferred_element_type=jnp.float32
    )


def against_cols(left, right):
    return lax.dot_general(
        left, right, (((1,), (1,)), ((), ())), preferred_element_type=jnp.float32
    )


def per_device(tokens, grad_out, routes, gates, w_gate, w_up, w_down):
    tok_count, model_width = tokens.shape
    route_count = routes.shape[1]
    expert_count = lax.axis_size("exp")
    slot_cap = max(2, 2 * tok_count * route_count // expert_count)
    route_total = tok_count * route_count
    slot_total = expert_count * slot_cap
    flat_routes = routes.reshape(-1)
    onehot = (flat_routes[:, None] == jnp.arange(expert_count, dtype=jnp.int32)[None, :]).astype(
        jnp.int32
    )
    slot_rank = jnp.sum((jnp.cumsum(onehot, axis=0) - 1) * onehot, axis=1)
    slot_index = flat_routes * slot_cap + slot_rank
    source = (
        jnp.full((slot_total,), route_total, jnp.int32)
        .at[slot_index]
        .set(jnp.arange(route_total, dtype=jnp.int32))
    )
    scaled = (gates[:, :, None] * grad_out[:, None, :].astype(jnp.float32)).astype(jnp.bfloat16)
    scaled = scaled.reshape(route_total, model_width)
    zero_row = jnp.zeros((1, model_width), jnp.bfloat16)
    tok_pad = jnp.concatenate([tokens, zero_row], axis=0)
    scaled_pad = jnp.concatenate([scaled, zero_row], axis=0)
    tok_source = jnp.where(source < route_total, source // route_count, tok_count)
    x_send = tok_pad[tok_source]
    g_send = scaled_pad[source]
    x_recv, g_recv = (
        lax.all_to_all(x_send, "exp", split_axis=0, concat_axis=0, tiled=True),
        lax.all_to_all(g_send, "exp", split_axis=0, concat_axis=0, tiled=True),
    )
    full_gate, full_up, full_down = (
        lax.all_gather(w_gate[0], "rep", axis=0, tiled=True),
        lax.all_gather(w_up[0], "rep", axis=0, tiled=True),
        lax.all_gather(w_down[0], "rep", axis=0, tiled=True),
    )
    pre_gate = jnp.dot(x_recv, full_gate, preferred_element_type=jnp.float32)
    pre_up = jnp.dot(x_recv, full_up, preferred_element_type=jnp.float32)
    hid_grad = jnp.dot(g_recv, full_down, preferred_element_type=jnp.float32)
    sig_gate = jax.nn.sigmoid(pre_gate)
    silu_gate = pre_gate * sig_gate
    hidden = (silu_gate * pre_up).astype(jnp.bfloat16)
    d_gate = (hid_grad * pre_up * sig_gate * (1.0 + pre_gate * (1.0 - sig_gate))).astype(
        jnp.bfloat16
    )
    d_up = (hid_grad * silu_gate).astype(jnp.bfloat16)
    row_grad = (against_cols(d_gate, full_gate) + against_cols(d_up, full_up)).astype(jnp.bfloat16)
    returned = lax.all_to_all(row_grad, "exp", split_axis=0, concat_axis=0, tiled=True)
    picked = returned[slot_index].reshape(tok_count, route_count, model_width)
    grad_in = jnp.sum(picked.astype(jnp.float32), axis=1).astype(jnp.bfloat16)
    summed = lax.psum_scatter(
        jnp.stack(
            [
                contract_rows(x_recv, d_gate),
                contract_rows(x_recv, d_up),
                contract_rows(g_recv, hidden),
            ],
            axis=1,
        ),
        "rep",
        scatter_dimension=0,
        tiled=True,
    )
    grad_gate = summed[:, 0, :]
    grad_up = summed[:, 1, :]
    grad_down = summed[:, 2, :]
    return (grad_gate[None], grad_up[None], grad_down[None], grad_in)


def solution(mesh):
    placed = (
        P(("rep", "exp"), None),
        P(("rep", "exp"), None),
        P(("rep", "exp"), None),
        P(("rep", "exp"), None),
        P("exp", "rep", None),
        P("exp", "rep", None),
        P("exp", "rep", None),
    )
    return jax.shard_map(
        per_device,
        mesh=mesh,
        in_specs=placed,
        out_specs=(
            P("exp", "rep", None),
            P("exp", "rep", None),
            P("exp", "rep", None),
            P(("rep", "exp"), None),
        ),
        check_vma=False,
    )
```

profile of v0, /device:TPU:0, one launch (start us, length us, event | category | flops | bytes accessed | tf_op | source)
XLA Modules:
  0.0 352.3 jit_solution(11204724826656335633)
XLA Ops:
  7.2 0.7 all-gather.9.cloned.1.call-update
  8.0 0.7 all-gather.7.cloned.1.call-update
  8.7 0.8 copy.12
  9.7 0.7 broadcast_multiply_fusion
  11.7 1.4 scatter_custom_fusion
  13.1 3.3 gather_fusion
  16.4 6.5 %all-to-all-start = ((bf16[8,64,2048]{2,1,0:T(8,128)(2,1)}), bf16[8,64,2048]{2,1,0:T(8,128)(2,1)}, u32[]{:S(2)}, u32[]{:S(2)}) async-start(bf16[8,64,2048]{2,1,0:T(8,128)(2,1)} %bitcast.4), calls=%async_computation | async-start | bytes 4194304 | tf_op jit(solution)/shard_map/all_to_all | solution.py:46
  23.9 1.0 mul.64
  25.0 2.5 mul.65
  27.5 1.8 multiply_convert_fusion
  29.4 3.4 gather_fusion.1
  32.7 39.3 %all-to-all-done = bf16[8,64,2048]{2,1,0:T(8,128)(2,1)} async-done(((bf16[8,64,2048]{2,1,0:T(8,128)(2,1)}), bf16[8,64,2048]{2,1,0:T(8,128)(2,1)}, u32[]{:S(2)}, u32[]{:S(2)}) %all-to-all-start) | async-done | bytes 2097184 | tf_op jit(solution)/shard_map/all_to_all | solution.py:46
  72.1 3.6 %all-to-all-start.1 = ((bf16[8,64,2048]{2,1,0:T(8,128)(2,1)}), bf16[8,64,2048]{2,1,0:T(8,128)(2,1)S(1)}, u32[]{:S(2)}, u32[]{:S(2)}) async-start(bf16[8,64,2048]{2,1,0:T(8,128)(2,1)} %bitcast.6), calls=%async_computation.1 | async-start | bytes 4194304 | tf_op jit(solution)/shard_map/all_to_all | solution.py:47
  75.9 5.5 %fusion.6 = f32[512,768]{1,0:T(8,128)} fusion(bf16[512,2048]{1,0:T(8,128)(2,1)} %bitcast.5, bf16[1,2048,768]{2,1,0:T(8,128)(2,1)} %all-gather.9.cloned.1.call-done), kind=kOutput, calls=%fused_computation.15 | convolution fusion | flops 1610612736 | bytes 6815744 | tf_op jit(solution)/shard_map/dot_general | solution.py:55
  81.4 43.3 %all-to-all-done.1 = bf16[8,64,2048]{2,1,0:T(8,128)(2,1)S(1)} async-done(((bf16[8,64,2048]{2,1,0:T(8,128)(2,1)}), bf16[8,64,2048]{2,1,0:T(8,128)(2,1)S(1)}, u32[]{:S(2)}, u32[]{:S(2)}) %all-to-all-start.1) | async-done | bytes 2097184 | tf_op jit(solution)/shard_map/all_to_all | solution.py:47
  124.7 4.8 %fusion.8 = f32[512,768]{1,0:T(8,128)} fusion(bf16[512,2048]{1,0:T(8,128)(2,1)S(1)} %bitcast.55, bf16[1,2048,768]{2,1,0:T(8,128)(2,1)} %all-gather.7.cloned.1.call-done), kind=kOutput, calls=%fused_computation.17 | convolution fusion | flops 1610612736 | bytes 6815744 | tf_op jit(solution)/shard_map/dot_general | solution.py:56
  129.5 18.8 %all-gather.11.cloned.1.call-done = bf16[1,2048,768]{2,1,0:T(8,128)(2,1)} async-done(((bf16[1,512,768]{2,1,0:T(8,128)(2,1)}), bf16[1,2048,768]{2,1,0:T(8,128)(2,1)}) %all-gather.11.cloned.1.call-update) | async-done | bytes 3145744 | tf_op jit(solution)/shard_map/all_gather | solution.py:50
  148.3 5.8 %multiply_convert_fusion.3 = (bf16[512,768]{1,0:T(8,128)(2,1)S(1)}, bf16[512,768]{1,0:T(8,128)(2,1)S(1)}, f32[512,768]{1,0:T(8,128)S(1)}) fusion(f32[512,768]{1,0:T(8,128)} %fusion.8, f32[512,768]{1,0:T(8,128)} %fusion.6, bf16[512,2048]{1,0:T(8,128)(2,1)} %bitcast.5, bf16[1,2048,768]{2,1,0:T(8,128)(2,1)} %all-gather.11.cloned.1.call-done), kind=kOutput, calls=%fused_computation.25 | convolution fusion | flops 1615724544 | bytes 11534336 | tf_op jit(solution)/shard_map/dot_general | solution.py:54
  154.1 2.0 convolution_bitcast_fusion
  156.2 3.5 convolution_bitcast_fusion.1
  159.7 3.5 convolution_bitcast_fusion.2
  163.2 6.9 %pad_maximum_fusion = f32[2048,3,768]{2,0,1:T(8,128)} fusion(f32[2048,1,768]{2,0,1:T(8,128)S(1)} %convolution_bitcast_fusion, f32[2048,1,768]{2,0,1:T(8,128)S(1)} %convolution_bitcast_fusion.1, f32[2048,1,768]{2,0,1:T(8,128)S(1)} %convolution_bitcast_fusion.2), kind=kLoop, calls=%fused_computation.4 | loop fusion | flops 9437184 | bytes 37748736 | tf_op jit(solution)/shard_map/stack | solution.py:69
  170.1 1.9 copy-done.4
  172.0 3.1 fusion
  175.1 3.2 add_convert_fusion
  178.3 4.6 %all-to-all-start.2 = ((bf16[8,64,2048]{2,1,0:T(8,128)(2,1)}), bf16[8,64,2048]{2,1,0:T(8,128)(2,1)S(1)}, u32[]{:S(2)}, u32[]{:S(2)}) async-start(bf16[8,64,2048]{2,1,0:T(8,128)(2,1)} %bitcast.57), calls=%async_computation.3 | async-start | bytes 4194304 | tf_op jit(solution)/shard_map/all_to_all | solution.py:65
  183.0 49.1 %all-to-all-done.2 = bf16[8,64,2048]{2,1,0:T(8,128)(2,1)S(1)} async-done(((bf16[8,64,2048]{2,1,0:T(8,128)(2,1)}), bf16[8,64,2048]{2,1,0:T(8,128)(2,1)S(1)}, u32[]{:S(2)}, u32[]{:S(2)}) %all-to-all-start.2) | async-done | bytes 2097184 | tf_op jit(solution)/shard_map/all_to_all | solution.py:65
  232.0 1.4 gather_fusion.2
  233.4 0.7 reshape.73
  234.1 3.7 %reduce_sum.25 = bf16[128,2048]{1,0:T(8,128)(2,1)} reduce(bf16[128,2,2048]{2,1,0:T(2,128)(2,1)S(1)} %reshape.73, bf16[]{:T(256)} %constant.13.clone.1), dimensions={1}, to_apply=%region_5.6 | reduce | flops 262144 | bytes 1572866 | tf_op jit(solution)/shard_map/reduce_sum | solution.py:67
  237.8 103.3 %reduce-scatter.2.cloned.1.call-done = f32[512,3,768]{2,0,1:T(8,128)} async-done(((f32[2048,3,768]{2,0,1:T(8,128)}), f32[512,3,768]{2,0,1:T(8,128)}) %reduce-scatter.2.cloned.1.call-update) | async-done | bytes 4718608 | tf_op jit(solution)/shard_map/reduce_scatter | solution.py:68
  341.1 4.6 %slice_bitcast_fusion = (f32[1,512,768]{2,1,0:T(8,128)}, f32[1,512,768]{2,1,0:T(8,128)}, f32[1,512,768]{2,1,0:T(8,128)}) fusion(f32[512,3,768]{2,0,1:T(8,128)} %reduce-scatter.2.cloned.1.call-done), kind=kLoop, calls=%fused_computation.20 | loop fusion | bytes 9437184 | tf_op jit(solution)/shard_map/broadcast_in_dim;squeeze | solution.py:84
  (44 shorter events, 3.0 us)
Async XLA Ops:
  7.2 4.4 %copy-start.1 = (bf16[128,2048]{1,0:T(8,128)(2,1)S(1)}, bf16[128,2048]{1,0:T(8,128)(2,1)}, u32[]{:S(2)}) copy-start(bf16[128,2048]{1,0:T(8,128)(2,1)} %param.7) | copy-start | bytes 1572868
  7.2 68.8 %all-gather.9.cloned.1.call-start = ((), (), s32[]{:S(2)}) async-start(), calls=%async_computation.6 | async-start | bytes 3932160 | tf_op jit(solution)/shard_map/all_gather | solution.py:51
  7.9 116.8 %all-gather.7.cloned.1.call-start = ((), (), s32[]{:S(2)}) async-start(), calls=%async_computation.5 | async-start | bytes 3932160 | tf_op jit(solution)/shard_map/all_gather | solution.py:52
  16.4 7.2 %copy-start.2 = (f32[128,2]{0,1:T(2,128)S(1)}, f32[128,2]{0,1:T(2,128)}, u32[]{:S(2)}) copy-start(f32[128,2]{0,1:T(2,128)} %param.10) | copy-start | bytes 3076
  16.4 7.5 %copy-start = (bf16[128,2048]{1,0:T(8,128)(2,1)S(1)}, bf16[128,2048]{1,0:T(8,128)(2,1)}, u32[]{:S(2)}) copy-start(bf16[128,2048]{1,0:T(8,128)(2,1)} %param.8) | copy-start | bytes 1572868
  16.4 55.6 %all-to-all-start = ((bf16[8,64,2048]{2,1,0:T(8,128)(2,1)}), bf16[8,64,2048]{2,1,0:T(8,128)(2,1)}, u32[]{:S(2)}, u32[]{:S(2)}) async-start(bf16[8,64,2048]{2,1,0:T(8,128)(2,1)} %bitcast.4), calls=%async_computation | async-start | bytes 4194304 | tf_op jit(solution)/shard_map/all_to_all | solution.py:46
  22.9 125.4 %all-gather.11.cloned.1.call-start = ((), (), s32[]{:S(2)}) async-start(), calls=%async_computation.7 | async-start | bytes 3932160 | tf_op jit(solution)/shard_map/all_gather | solution.py:50
  72.1 52.6 %all-to-all-start.1 = ((bf16[8,64,2048]{2,1,0:T(8,128)(2,1)}), bf16[8,64,2048]{2,1,0:T(8,128)(2,1)S(1)}, u32[]{:S(2)}, u32[]{:S(2)}) async-start(bf16[8,64,2048]{2,1,0:T(8,128)(2,1)} %bitcast.6), calls=%async_computation.1 | async-start | bytes 4194304 | tf_op jit(solution)/shard_map/all_to_all | solution.py:47
  75.7 265.4 %reduce-scatter.2.cloned.1.call-start = ((), (), s32[]{:S(2)}) async-start(), calls=%async_computation.4 | async-start | bytes 23592960 | tf_op jit(solution)/shard_map/reduce_scatter | solution.py:68
  148.3 5.8 %copy-start.8 = (f32[512,768]{1,0:T(8,128)S(1)}, f32[512,768]{1,0:T(8,128)}, u32[]{:S(2)}) copy-start(f32[512,768]{1,0:T(8,128)} %fusion.6) | copy-start | bytes 4718596
  154.1 2.1 copy-start.5
  154.1 5.6 %copy-start.7 = (bf16[512,768]{1,0:T(8,128)(2,1)}, bf16[512,768]{1,0:T(8,128)(2,1)S(1)}, u32[]{:S(2)}) copy-start(bf16[512,768]{1,0:T(8,128)(2,1)S(1)} %get-tuple-element.7) | copy-start | bytes 2359300
  170.1 1.9 copy-start.4
  172.0 3.1 copy-start.3
  172.0 3.1 copy-start.6
  178.3 53.7 %all-to-all-start.2 = ((bf16[8,64,2048]{2,1,0:T(8,128)(2,1)}), bf16[8,64,2048]{2,1,0:T(8,128)(2,1)S(1)}, u32[]{:S(2)}, u32[]{:S(2)}) async-start(bf16[8,64,2048]{2,1,0:T(8,128)(2,1)} %bitcast.57), calls=%async_computation.3 | async-start | bytes 4194304 | tf_op jit(solution)/shard_map/all_to_all | solution.py:65
Sparse Core Ops, SparseCore 0:
  9.8 46.6 all-gather.8
  58.4 43.9 all-gather.6
  104.3 43.9 all-gather.10
  170.2 170.8 reduce-scatter.1
where the time goes:
time: 353 us; the launch traced here: 352 us
  waiting for transfers between devices  256 us (73%)
  matrix products  31.4 us (9%)
  local copies, waits for them, and re-layouts  22.2 us (6%)
  starting transfers between devices  15 us (4%)
  between operations  14 us (4%)
  other arithmetic  13.8 us (4%)
    reduce_scatter x1, waiting for transfers between devices, per_device(): lax.psum_scatter(jnp.stack([contract_rows(x_recv, d_gate), contract_rows(...  103 us
    all_to_all x1, waiting for transfers between devices, per_device(): lax.all_to_all(row_grad, 'exp', split_axis=0, concat_axis=0, tiled=True)  49.1 us
    all_to_all x1, waiting for transfers between devices, per_device(): lax.all_to_all(g_send, 'exp', split_axis=0, concat_axis=0, tiled=True)  43.3 us
    all_to_all x1, waiting for transfers between devices, per_device(): lax.all_to_all(x_send, 'exp', split_axis=0, concat_axis=0, tiled=True)  39.3 us
    all_gather x1, waiting for transfers between devices, per_device(): lax.all_gather(w_gate[0], 'rep', axis=0, tiled=True)  18.8 us
    dot_general x3, matrix products, contract_rows(): lax.dot_general(left, right, (((0,), (0,)), ((), ())), preferred_element_...  9 us
  transfers between devices with their start and end apart: 7, of which 5 were waited for; matrix products, arithmetic and copies ran while one was open for 11% of the time, Pallas kernels for 0%

commit v1 on v0

v1 whole, which is shorter than its diff:
```python
import functools

import jax
import jax.numpy as jnp
from jax import lax
from jax.experimental import pallas as pl
from jax.experimental.pallas import tpu as pltpu
from jax.sharding import PartitionSpec as P

MESH = pl.DeviceIdType.MESH
F32 = jnp.float32
BF16 = jnp.bfloat16


def contract_rows(left, right):
    return lax.dot_general(left, right, (((0,), (0,)), ((), ())), preferred_element_type=F32)


def against_cols(left, right):
    return lax.dot_general(left, right, (((1,), (1,)), ((), ())), preferred_element_type=F32)


def remote(src, dst, send_sem, recv_sem, rep, exp):
    return pltpu.make_async_remote_copy(
        src_ref=src,
        dst_ref=dst,
        send_sem=send_sem,
        recv_sem=recv_sem,
        device_id=(rep, exp),
        device_id_type=MESH,
    )


def greet(rep, exp, x_rep, y_rep, exp_count):
    barrier = pltpu.get_barrier_semaphore()
    for step in range(1, exp_count):
        other = lax.rem(exp + step, exp_count)
        pl.semaphore_signal(barrier, inc=1, device_id=(rep, other), device_id_type=MESH)
    for other in (x_rep, y_rep):
        pl.semaphore_signal(barrier, inc=1, device_id=(other, exp), device_id_type=MESH)
    pl.semaphore_wait(barrier, exp_count + 1)


def rep_neighbours(rep):
    return rep + 1 - 2 * lax.rem(rep, 2), lax.rem(rep + 2, 4), 3 - rep


def gather_kernel(
    tok, grd, info, wg, wu, wd,
    tok_o, grd_o, info_o, wg_o, wu_o, wd_o,
    row_send, row_recv, info_send, info_recv, w_send, w_fwd, w_recv, local_sem,
):
    rep, exp = lax.axis_index("rep"), lax.axis_index("exp")
    x_rep, y_rep, diag = rep_neighbours(rep)
    z, core = lax.div(exp, 2), lax.rem(exp, 2)
    sibling = exp + 1 - 2 * core
    greet(rep, exp, x_rep, y_rep, 8)

    rows_in, rows_out = (tok, grd), (tok_o, grd_o)
    w_in, w_out = (wg, wu, wd), (wg_o, wu_o, wd_o)
    half = wg.shape[0] // 2
    part = (pl.ds(0, half), pl.ds(half, half))
    targets = (exp + 2, exp - 2, sibling)

    def row_copy(a, block, way, own):
        dst = rows_out[a].at[block]
        return remote(
            rows_in[a] if own else dst, dst,
            row_send.at[a, lax.div(block, 2), way], row_recv.at[a, block], rep, targets[way],
        )

    def row_ways(block, own, up, down, act):
        for a in range(2):
            if up:
                pl.when(z < 3)(lambda a=a: act(row_copy(a, block, 0, own)))
            if down:
                pl.when(z > 0)(lambda a=a: act(row_copy(a, block, 1, own)))
            act(row_copy(a, block, 2, own))

    def start(copy):
        copy.start()

    def sent(copy):
        copy.wait_send()

    def w_own(k, h, way):
        return remote(
            w_in[k].at[part[h]], w_out[k].at[rep, part[h]],
            w_send.at[k, h, way], w_recv.at[k, rep, h], (x_rep, y_rep)[way], exp,
        )

    def w_forward(k, way):
        block, h, to = ((x_rep, 0, y_rep), (y_rep, 1, x_rep))[way]
        ref = w_out[k].at[block, part[h]]
        return remote(ref, ref, w_fwd.at[k, way], w_recv.at[k, block, h], to, exp)

    def w_arrived(k, block, h):
        ref = w_out[k].at[block, part[h]]
        remote(ref, ref, w_fwd.at[k, 0], w_recv.at[k, block, h], y_rep, exp).wait_recv()

    def info_copy(step):
        other = lax.rem(exp + step, 8)
        return remote(
            info, info_o.at[exp], info_send.at[step - 1], info_recv.at[exp], rep, other
        )

    row_ways(exp, True, True, True, start)
    for h in range(2):
        for k in range(3):
            w_own(k, h, 0).start()
            w_own(k, 1 - h, 1).start()
    for step in range(1, 8):
        info_copy(step).start()
    local = [
        pltpu.make_async_copy(tok, tok_o.at[exp], local_sem.at[0]),
        pltpu.make_async_copy(grd, grd_o.at[exp], local_sem.at[1]),
        pltpu.make_async_copy(info, info_o.at[exp], local_sem.at[2]),
        pltpu.make_async_copy(wg, wg_o.at[rep], local_sem.at[3]),
        pltpu.make_async_copy(wu, wu_o.at[rep], local_sem.at[4]),
        pltpu.make_async_copy(wd, wd_o.at[rep], local_sem.at[5]),
    ]
    for copy in local:
        copy.start()

    for s in range(1, 4):
        @pl.when(z >= s)
        def _():
            block = exp - 2 * s
            for a in range(2):
                row_copy(a, block, 2, False).wait_recv()
            row_ways(block, False, True, False, start)

        @pl.when(z + s <= 3)
        def _():
            block = exp + 2 * s
            for a in range(2):
                row_copy(a, block, 2, False).wait_recv()
            row_ways(block, False, False, True, start)

        if s == 1:
            for k in range(3):
                w_arrived(k, x_rep, 0)
                w_forward(k, 0).start()
                w_arrived(k, y_rep, 1)
                w_forward(k, 1).start()

    for k in range(3):
        w_arrived(k, x_rep, 1)
        w_arrived(k, y_rep, 0)
        w_arrived(k, diag, 0)
        w_arrived(k, diag, 1)
    for j in range(4):
        for a in range(2):
            row_copy(a, 2 * j + 1 - core, 2, False).wait_recv()
    for step in range(1, 8):
        block = lax.rem(exp + step, 8)
        remote(
            info, info_o.at[block], info_send.at[step - 1], info_recv.at[block], rep, block
        ).wait_recv()
    for copy in local:
        copy.wait()
    row_ways(exp, True, True, True, sent)
    for s in range(1, 4):
        pl.when(z >= s)(lambda s=s: row_ways(exp - 2 * s, False, True, False, sent))
        pl.when(z + s <= 3)(lambda s=s: row_ways(exp + 2 * s, False, False, True, sent))
    for k in range(3):
        for way in range(2):
            for h in range(2):
                w_own(k, h, way).wait_send()
            w_forward(k, way).wait_send()
    for step in range(1, 8):
        info_copy(step).wait_send()


def scatter_kernel(
    back, pg, pu, pd,
    back_o, rg, ru, rd,
    tmp, summed, back_send, back_recv, p_send, p_recv, local_sem,
):
    rep, exp = lax.axis_index("rep"), lax.axis_index("exp")
    x_rep, y_rep, diag = rep_neighbours(rep)
    greet(rep, exp, x_rep, y_rep, 8)
    terms, received = (pg, pu, pd), (rg, ru, rd)
    half = pg.shape[1] // 2
    part = (pl.ds(0, half), pl.ds(half, half))
    near = (x_rep, y_rep)

    def relay(k, way):
        return remote(
            terms[k].at[diag, part[way]], tmp.at[k, way],
            p_send.at[k, way, 0], p_recv.at[k, way, 0], near[way], exp,
        )

    def direct(k, way):
        return remote(
            terms[k].at[near[way], part[way]], received[k].at[way, part[way]],
            p_send.at[k, way, 1], p_recv.at[k, way, 1], near[way], exp,
        )

    def onward(k, way):
        return remote(
            summed.at[k, way], received[k].at[way, part[1 - way]],
            p_send.at[k, way, 2], p_recv.at[k, way, 2], near[way], exp,
        )

    def back_copy(step):
        other = lax.rem(exp + step, 8)
        return remote(
            back.at[other], back_o.at[exp], back_send.at[step - 1], back_recv.at[exp], rep, other
        )

    for k in range(3):
        for way in range(2):
            relay(k, way).start()
    for step in (4, 3, 5, 2, 6, 1, 7):
        back_copy(step).start()
    for k in range(3):
        for way in range(2):
            direct(k, way).start()
    own = pltpu.make_async_copy(back.at[exp], back_o.at[exp], local_sem)
    own.start()
    for k in range(3):
        for way in range(2):
            relay(k, way).wait_recv()
            rows = 64

            @pl.loop(0, half // rows)
            def _(i):
                at = pl.ds(pl.multiple_of(i * rows, rows), rows)
                mine = terms[k][
                    near[1 - way], pl.ds(pl.multiple_of(way * half + i * rows, rows), rows), :
                ]
                summed[k, 1 - way, at, :] = (
                    mine.astype(F32) + tmp[k, way, at, :].astype(F32)
                ).astype(BF16)

            onward(k, 1 - way).start()
    own.wait()
    for k in range(3):
        for way in range(2):
            direct(k, way).wait_recv()
            onward(k, way).wait_recv()
    for step in range(1, 8):
        block = lax.rem(exp + step, 8)
        remote(
            back.at[block], back_o.at[block], back_send.at[step - 1], back_recv.at[block], rep,
            block,
        ).wait_recv()
    for k in range(3):
        for way in range(2):
            relay(k, way).wait_send()
            direct(k, way).wait_send()
            onward(k, way).wait_send()
    for step in range(1, 8):
        back_copy(step).wait_send()


ANY = pl.BlockSpec(memory_space=pl.ANY)
VMEM = pl.BlockSpec(memory_space=pltpu.VMEM)
DMA = pltpu.SemaphoreType.DMA


def gather_all(tokens, grad_out, info, w_gate, w_up, w_down):
    rows = jax.ShapeDtypeStruct((8,) + tokens.shape, BF16)
    weights = jax.ShapeDtypeStruct((4,) + w_gate.shape, BF16)
    return pl.pallas_call(
        gather_kernel,
        out_shape=(rows, rows, jax.ShapeDtypeStruct((8,) + info.shape, F32)) + (weights,) * 3,
        in_specs=[ANY] * 6,
        out_specs=(ANY,) * 6,
        scratch_shapes=[
            DMA((2, 4, 3)), DMA((2, 8)), DMA((7,)), DMA((8,)),
            DMA((3, 2, 2)), DMA((3, 2)), DMA((3, 4, 2)), DMA((6,)),
        ],
        compiler_params=pltpu.CompilerParams(collective_id=0, has_side_effects=True),
    )(tokens, grad_out, info, w_gate, w_up, w_down)


def scatter_all(back, p_gate, p_up, p_down):
    _, depth, width = p_gate.shape
    got = jax.ShapeDtypeStruct((2, depth, width), BF16)
    return pl.pallas_call(
        scatter_kernel,
        out_shape=(jax.ShapeDtypeStruct(back.shape, BF16), got, got, got),
        in_specs=[ANY] + [VMEM] * 3,
        out_specs=(ANY,) * 4,
        scratch_shapes=[
            pltpu.VMEM((3, 2, depth // 2, width), BF16),
            pltpu.VMEM((3, 2, depth // 2, width), BF16),
            DMA((7,)), DMA((8,)), DMA((3, 2, 3)), DMA((3, 2, 3)), DMA,
        ],
        compiler_params=pltpu.CompilerParams(
            collective_id=1, has_side_effects=True, vmem_limit_bytes=32 * 1024 * 1024
        ),
    )(back, p_gate, p_up, p_down)


def expert_math(x_rows, g_rows, full_gate, full_up, full_down):
    pre_gate = jnp.dot(x_rows, full_gate, preferred_element_type=F32)
    pre_up = jnp.dot(x_rows, full_up, preferred_element_type=F32)
    hid_grad = jnp.dot(g_rows, full_down, preferred_element_type=F32)
    sig_gate = jax.nn.sigmoid(pre_gate)
    silu_gate = pre_gate * sig_gate
    hidden = (silu_gate * pre_up).astype(BF16)
    d_gate = (hid_grad * pre_up * sig_gate * (1.0 + pre_gate * (1.0 - sig_gate))).astype(BF16)
    d_up = (hid_grad * silu_gate).astype(BF16)
    row_grad = (against_cols(d_gate, full_gate) + against_cols(d_up, full_up)).astype(BF16)
    return hidden, d_gate, d_up, row_grad


def ranks_of(named):
    count = named.shape[-1]
    earlier = (jnp.arange(count)[:, None] < jnp.arange(count)[None, :]).astype(BF16)
    return jnp.dot(named.astype(BF16), earlier, preferred_element_type=F32).astype(jnp.int32)


def slots_of(routes, expert_count, slot_cap):
    tok_count = routes.shape[0]
    experts = jnp.arange(expert_count, dtype=jnp.int32)[:, None]
    named = (routes[:, 0][None, :] == experts) | (routes[:, 1][None, :] == experts)
    rank = jnp.where(named, ranks_of(named), slot_cap)
    held = rank[:, None, :] == jnp.arange(slot_cap, dtype=jnp.int32)[None, :, None]
    return held.reshape(expert_count * slot_cap, tok_count)


def block_of_mesh(tokens, grad_out, routes, gates, w_gate, w_up, w_down):
    tok_count, model_width = tokens.shape
    depth, width = w_gate.shape[1:]
    expert_count = lax.axis_size("exp")
    slot_cap = max(2, 2 * tok_count * routes.shape[1] // expert_count)
    rep, exp = lax.axis_index("rep"), lax.axis_index("exp")
    info = jnp.concatenate(
        [routes.T.astype(F32), gates.T, jnp.zeros((4, tok_count), F32)], axis=0
    )
    all_tok, all_grd, all_info, full_gate, full_up, full_down = gather_all(
        tokens, grad_out, info, w_gate[0], w_up[0], w_down[0]
    )
    full_gate, full_up, full_down = (
        w.reshape(4 * depth, width) for w in (full_gate, full_up, full_down)
    )
    mine = exp.astype(F32)
    first, second = all_info[:, 0, :] == mine, all_info[:, 1, :] == mine
    named = first | second
    gate = jnp.where(first, all_info[:, 2, :], jnp.where(second, all_info[:, 3, :], 0.0))
    rank = jnp.where(named, ranks_of(named), slot_cap)
    held = rank[:, None, :] == jnp.arange(slot_cap, dtype=jnp.int32)[None, :, None]
    pick = held.astype(BF16)
    slot_gate = jnp.sum(jnp.where(held, gate[:, None, :], 0.0), axis=2)
    into = functools.partial(
        lax.dot_general,
        dimension_numbers=(((2,), (1,)), ((0,), (0,))),
        preferred_element_type=F32,
    )
    x_rows = into(pick, all_tok).astype(BF16).reshape(expert_count * slot_cap, model_width)
    g_rows = (slot_gate[:, :, None] * into(pick, all_grd)).astype(BF16)
    g_rows = g_rows.reshape(expert_count * slot_cap, model_width)
    hidden, d_gate, d_up, row_grad = expert_math(x_rows, g_rows, full_gate, full_up, full_down)
    pairs = ((x_rows, d_gate), (x_rows, d_up), (g_rows, hidden))
    terms = [contract_rows(a, b).astype(BF16).reshape(4, depth, width) for a, b in pairs]
    returned, *received = scatter_all(
        row_grad.reshape(expert_count, slot_cap, model_width), *terms
    )
    grads = [
        contract_rows(lax.dynamic_slice_in_dim(a, rep * depth, depth, 1), b)
        + got[0].astype(F32) + got[1].astype(F32)
        for (a, b), got in zip(pairs, received)
    ]
    slots = slots_of(routes, expert_count, slot_cap).astype(BF16)
    grad_in = contract_rows(
        slots, returned.reshape(expert_count * slot_cap, model_width)
    ).astype(BF16)
    return (*(g[None] for g in grads), grad_in)


def any_mesh(tokens, grad_out, routes, gates, w_gate, w_up, w_down):
    tok_count, _ = tokens.shape
    expert_count = lax.axis_size("exp")
    slot_cap = max(2, 2 * tok_count * routes.shape[1] // expert_count)
    slots = slots_of(routes, expert_count, slot_cap)
    owner = jnp.repeat(jnp.arange(expert_count, dtype=jnp.int32), slot_cap)[:, None]
    pick = slots.astype(BF16)
    gate = jnp.where(routes[:, 0][None, :] == owner, gates[:, 0][None, :], gates[:, 1][None, :])
    slot_gate = jnp.sum(jnp.where(slots, gate, 0.0), axis=1)
    x_send = jnp.dot(pick, tokens, preferred_element_type=F32).astype(BF16)
    g_send = jnp.dot(pick, grad_out, preferred_element_type=F32)
    g_send = (slot_gate[:, None] * g_send).astype(BF16)
    x_rows = lax.all_to_all(x_send, "exp", split_axis=0, concat_axis=0, tiled=True)
    g_rows = lax.all_to_all(g_send, "exp", split_axis=0, concat_axis=0, tiled=True)
    full = [lax.all_gather(w[0], "rep", axis=0, tiled=True) for w in (w_gate, w_up, w_down)]
    hidden, d_gate, d_up, row_grad = expert_math(x_rows, g_rows, *full)
    returned = lax.all_to_all(row_grad, "exp", split_axis=0, concat_axis=0, tiled=True)
    grad_in = contract_rows(pick, returned).astype(BF16)
    grads = [
        lax.psum_scatter(contract_rows(a, b), "rep", scatter_dimension=0, tiled=True)[None]
        for a, b in ((x_rows, d_gate), (x_rows, d_up), (g_rows, hidden))
    ]
    return (*grads, grad_in)


def solution(mesh):
    rows = P(("rep", "exp"), None)
    weights = P("exp", "rep", None)
    kernels = mesh.shape["rep"] == 4 and mesh.shape["exp"] == 8
    return jax.shard_map(
        block_of_mesh if kernels else any_mesh,
        mesh=mesh,
        in_specs=(rows,) * 4 + (weights,) * 3,
        out_specs=(weights,) * 3 + (rows,),
        check_vma=False,
    )
```

time: 353 us -> 231 us (0.65)
  waiting for transfers between devices: 256 us -> 0 us
  Pallas kernels: 0 us -> 191 us
  local copies, waits for them, and re-layouts: 22.2 us -> 6.3 us
  starting transfers between devices: 15 us -> 0 us
  between operations: 14 us -> 0.83 us
  other arithmetic: 13.8 us -> 3.03 us
    pallas_call x0 -> x2, Pallas kernels: none -> 191 us  [the longest x1 111 us: gather_all(): pl.pallas_call(gather_kernel, out_shape=(rows, rows, jax.ShapeDtypeStruct...]
    all_to_all x3 -> x0, waiting for transfers between devices: 132 us -> none  [the longest x1 49.1 us: per_device(): lax.all_to_all(row_grad, 'exp', split_axis=0, concat_axis=0, tiled=True)]
    reduce_scatter x1 -> x0, waiting for transfers between devices: 103 us -> none  [per_device(): lax.psum_scatter(jnp.stack([contract_rows(x_recv, d_gate), contract_rows(...]
    all_gather x3 -> x0, waiting for transfers between devices: 18.8 us -> none  [the longest x1 18.8 us: per_device(): lax.all_gather(w_gate[0], 'rep', axis=0, tiled=True)]
    all_to_all x3 -> x0, starting transfers between devices: 14.7 us -> none  [the longest x1 6.46 us: per_device(): lax.all_to_all(x_send, 'exp', split_axis=0, concat_axis=0, tiled=True)]
    gather x3 -> x0, local copies, waits for them, and re-layouts: 8.04 us -> none  [the longest x1 3.38 us: per_device(): g_send = scaled_pad[source]]
    another operation x3 -> x0, other arithmetic: 7.55 us -> none  [the longest x1 6.93 us: per_device(): jnp.stack([contract_rows(x_recv, d_gate), contract_rows(x_recv, d_up), co...]
    dot_general x3 -> x7, matrix products: 9 us -> 16.4 us  [contract_rows(): lax.dot_general(left, right, (((0,), (0,)), ((), ())), preferred_element_...]
  transfers between devices with their start and end apart: 7 -> 0, of which waited for: 5 -> 0; matrix products, arithmetic and copies ran while one was open for 11% -> 0% of each run, Pallas kernels for 0% -> 0%
where the time goes in v1:
time: 231 us
  Pallas kernels  191 us (83%)
  matrix products  30 us (13%)
  local copies, waits for them, and re-layouts  6.3 us (3%)
  other arithmetic  3.03 us (1%)
    pallas_call x1, Pallas kernels, gather_all(): pl.pallas_call(gather_kernel, out_shape=(rows, rows, jax.ShapeDtypeStruct...  111 us
    pallas_call x1, Pallas kernels, scatter_all(): pl.pallas_call(scatter_kernel, out_shape=(jax.ShapeDtypeStruct(back.shape...  80.4 us
    dot_general x7, matrix products, contract_rows(): lax.dot_general(left, right, (((0,), (0,)), ((), ())), preferred_element_...  16.4 us
    unnamed x32, local copies, waits for them, and re-layouts  6.21 us

profile of v1, /device:TPU:0, one launch (start us, length us, event | category | flops | bytes accessed | tf_op | source)
XLA Modules:
  0.0 231.1 jit_solution(2671896032722897243)
XLA Ops:
  0.6 0.7 convert_bitcast_fusion
  1.3 0.1 pad.2.clone
  1.4 1.3 maximum_maximum_fusion.info
  2.7 110.5 %shard_map.102 = (bf16[8,128,2048]{2,1,0:T(8,128)(2,1)}, bf16[8,128,2048]{2,1,0:T(8,128)(2,1)}, f32[8,8,128]{2,1,0:T(8,128)}, bf16[4,512,768]{2,1,0:T(8,128)(2,1...) custom-call(bf16[128,2048]{1,0:T(8,128)(2,1)} %tok.1, bf16[128,2048]{1,0:T(8,128)(2,1)} %grd.1, ...), custom_call_target="tpu_custom_call" | custom-call | tf_op jit(solution)/shard_map/pallas_call | solution.py:266
  113.3 0.8 compare_or_fusion
  114.1 0.1 fusion.6
  114.3 3.0 %convolution_convert_fusion.3 = bf16[8,64,2048]{2,1,0:T(8,128)(2,1)S(1)} fusion(bf16[8,128,2048]{2,1,0:T(8,128)(2,1)} %get-tuple-element.15, s32[8,128]{1,0:T(8,128)S(1)} %fusion.6), kind=kOutput, calls=%fused_computation.5 | convolution fusion | flops 269549568 | bytes 6295552 | tf_op jit(solution)/shard_map/dot_general | solution.py:354
  117.3 0.1 copy-done.11
  117.4 1.8 fusion.23
  119.3 0.1 select_reduce_fusion
  119.4 0.9 copy-done.5
  120.3 0.7 multiply_convert_fusion
  121.0 0.0 copy-start.6
  121.0 1.7 copy-done.12
  122.7 1.8 fusion.22
  124.5 0.1 copy-done.10
  124.6 2.3 multiply_convert_fusion.1
  126.9 1.8 fusion.24
  128.7 1.8 add_convert_fusion
  130.6 1.9 convolution_convert_fusion.2
  132.4 2.1 convolution_convert_fusion.1
  134.5 0.0 copy-done.6
  134.5 1.9 convolution_convert_fusion
  136.4 80.4 %shard_map.103 = (bf16[8,64,2048]{2,1,0:T(8,128)(2,1)S(1)}, bf16[2,512,768]{2,1,0:T(8,128)(2,1)S(1)}, bf16[2,512,768]{2,1,0:T(8,128)(2,1)S(1)}, bf16[2,512,768]{2,1,0:T(8,128)(2,1)S(1)}) custom-call(bf16[8,64,2048]{2,1,0:T(8,128)(2,1)S(1)} %bitcast.76, bf16[4,512,768]{2,1,0:T(8,128)(2,1)S(1)} %bitcast.73, bf16[4,512,768]{2,1,0:T(8,128)(2,1)S(1)} %bitcast.74, ...), custom_call_target="tpu_custom_call" | custom-call | tf_op jit(solution)/shard_map/pallas_call | solution.py:282
  216.8 1.2 copy-done
  218.0 1.1 copy-done.2
  219.1 1.1 copy-done.4
  220.3 3.7 %fusion.3 = f32[1,512,768]{2,1,0:T(8,128)} fusion(bf16[512,768]{1,0:T(8,128)(2,1)} %copy-done.15, bf16[2,512,768]{2,1,0:T(8,128)(2,1)} %copy-done.4, bf16[512,2048]{1,0:T(8,128)(2,1)} %bitcast.84, s32[]{:T(128)S(6)} %select_n.27), kind=kOutput, calls=%fused_computation.15 | convolution fusion | flops 404226048 | bytes 4456452 | tf_op jit(solution)/shard_map/dot_general | solution.py:16
  223.9 2.9 %fusion.2 = f32[1,512,768]{2,1,0:T(8,128)} fusion(bf16[512,768]{1,0:T(8,128)(2,1)S(1)} %copy-done.14, bf16[2,512,768]{2,1,0:T(8,128)(2,1)S(1)} %copy-done.3, bf16[512,2048]{1,0:T(8,128)(2,1)} %bitcast.85, s32[]{:T(128)S(6)} %select_n.27), kind=kOutput, calls=%fused_computation.12 | convolution fusion | flops 404226048 | bytes 4456452 | tf_op jit(solution)/shard_map/dot_general | solution.py:16
  226.9 2.8 %fusion.1 = f32[1,512,768]{2,1,0:T(8,128)} fusion(bf16[512,768]{1,0:T(8,128)(2,1)S(1)} %get-tuple-element.24, bf16[2,512,768]{2,1,0:T(8,128)(2,1)S(1)} %copy-done.1, bf16[512,2048]{1,0:T(8,128)(2,1)} %bitcast.79, s32[]{:T(128)S(6)} %select_n.27), kind=kOutput, calls=%fused_computation.9 | convolution fusion | flops 404226048 | bytes 4456452 | tf_op jit(solution)/shard_map/dot_general | solution.py:16
  229.7 0.1 fusion.5
  229.8 1.3 fusion
  (26 shorter events, 0.1 us)
Async XLA Ops:
  114.3 3.2 %copy-start.11 = (bf16[4,512,768]{2,1,0:T(8,128)(2,1)S(1)}, bf16[4,512,768]{2,1,0:T(8,128)(2,1)}, u32[]{:S(2)}) copy-start(bf16[4,512,768]{2,1,0:T(8,128)(2,1)} %get-tuple-element.19) | copy-start | bytes 9437188
  117.3 15.1 %copy-start.7 = (bf16[8,64,2048]{2,1,0:T(8,128)(2,1)}, bf16[8,64,2048]{2,1,0:T(8,128)(2,1)S(1)}, u32[]{:S(2)}) copy-start(bf16[8,64,2048]{2,1,0:T(8,128)(2,1)S(1)} %convolution_convert_fusion.3) | copy-start | bytes 6291460
  117.4 1.8 copy-start.8
  117.4 2.9 %copy-start.5 = (bf16[8,128,2048]{2,1,0:T(8,128)(2,1)S(1)}, bf16[8,128,2048]{2,1,0:T(8,128)(2,1)}, u32[]{:S(2)}) copy-start(bf16[8,128,2048]{2,1,0:T(8,128)(2,1)} %get-tuple-element.16) | copy-start | bytes 12582916
  120.3 2.4 %copy-start.12 = (bf16[4,512,768]{2,1,0:T(8,128)(2,1)S(1)}, bf16[4,512,768]{2,1,0:T(8,128)(2,1)}, u32[]{:S(2)}) copy-start(bf16[4,512,768]{2,1,0:T(8,128)(2,1)} %get-tuple-element.17) | copy-start | bytes 9437188
  121.0 13.5 %copy-start.6 = (bf16[8,64,2048]{2,1,0:T(8,128)(2,1)}, bf16[8,64,2048]{2,1,0:T(8,128)(2,1)S(1)}, u32[]{:S(2)}) copy-start(bf16[8,64,2048]{2,1,0:T(8,128)(2,1)S(1)} %multiply_convert_fusion) | copy-start | bytes 6291460
  122.7 1.9 copy-start.10
  126.9 3.7 %copy-start.15 = (bf16[512,768]{1,0:T(8,128)(2,1)}, bf16[512,768]{1,0:T(8,128)(2,1)S(1)}, u32[]{:S(2)}) copy-start(bf16[512,768]{1,0:T(8,128)(2,1)S(1)} %get-tuple-element.25) | copy-start | bytes 2359300
  126.9 5.6 %copy-start.13 = (bf16[512,768]{1,0:T(8,128)(2,1)}, bf16[512,768]{1,0:T(8,128)(2,1)S(1)}, u32[]{:S(2)}) copy-start(bf16[512,768]{1,0:T(8,128)(2,1)S(1)} %get-tuple-element.26) | copy-start | bytes 2359300
  216.8 1.2 copy-start
  218.0 1.1 copy-start.2
  219.1 1.1 copy-start.4
  220.3 3.7 %copy-start.3 = (bf16[2,512,768]{2,1,0:T(8,128)(2,1)S(1)}, bf16[2,512,768]{2,1,0:T(8,128)(2,1)}, u32[]{:S(2)}) copy-start(bf16[2,512,768]{2,1,0:T(8,128)(2,1)} %copy-done.2) | copy-start | bytes 4718596
  220.3 3.7 %copy-start.14 = (bf16[512,768]{1,0:T(8,128)(2,1)S(1)}, bf16[512,768]{1,0:T(8,128)(2,1)}, u32[]{:S(2)}) copy-start(bf16[512,768]{1,0:T(8,128)(2,1)} %copy-done.13) | copy-start | bytes 2359300
  223.9 2.9 %copy-start.1 = (bf16[2,512,768]{2,1,0:T(8,128)(2,1)S(1)}, bf16[2,512,768]{2,1,0:T(8,128)(2,1)}, u32[]{:S(2)}) copy-start(bf16[2,512,768]{2,1,0:T(8,128)(2,1)} %copy-done) | copy-start | bytes 4718596
  226.9 2.8 %copy-start.9 = (s32[128,2]{0,1:T(2,128)S(1)}, s32[128,2]{0,1:T(2,128)}, u32[]{:S(2)}) copy-start(s32[128,2]{0,1:T(2,128)} %param.9) | copy-start | bytes 3076

commit v2 on v1

--- a/solution.py
+++ b/solution.py
@@ -48,7 +48,8 @@
 def gather_kernel(
     tok, grd, info, wg, wu, wd,
     tok_o, grd_o, info_o, wg_o, wu_o, wd_o,
-    row_send, row_recv, info_send, info_recv, w_send, w_fwd, w_recv, local_sem,
+    row_send, row_recv, info_send, info_recv, w_send, w_fwd, w_recv, fetch_sem, local_sem,
+    *staged,
 ):
     rep, exp = lax.axis_index("rep"), lax.axis_index("exp")
     x_rep, y_rep, diag = rep_neighbours(rep)
@@ -111,16 +112,22 @@
             w_own(k, 1 - h, 1).start()
     for step in range(1, 8):
         info_copy(step).start()
+    kept = list(zip(
+        (tok, grd, info, wg, wu, wd),
+        staged,
+        (tok_o.at[exp], grd_o.at[exp], info_o.at[exp], wg_o.at[rep], wu_o.at[rep], wd_o.at[rep]),
+    ))
+    fetch = [
+        pltpu.make_async_copy(src, mid, fetch_sem.at[i]) for i, (src, mid, _) in enumerate(kept)
+    ]
     local = [
-        pltpu.make_async_copy(tok, tok_o.at[exp], local_sem.at[0]),
-        pltpu.make_async_copy(grd, grd_o.at[exp], local_sem.at[1]),
-        pltpu.make_async_copy(info, info_o.at[exp], local_sem.at[2]),
-        pltpu.make_async_copy(wg, wg_o.at[rep], local_sem.at[3]),
-        pltpu.make_async_copy(wu, wu_o.at[rep], local_sem.at[4]),
-        pltpu.make_async_copy(wd, wd_o.at[rep], local_sem.at[5]),
+        pltpu.make_async_copy(mid, dst, local_sem.at[i]) for i, (_, mid, dst) in enumerate(kept)
     ]
-    for copy in local:
+    for copy in fetch:
         copy.start()
+    for first, second in zip(fetch, local):
+        first.wait()
+        second.start()
 
     for s in range(1, 4):
         @pl.when(z >= s)
@@ -175,7 +182,7 @@
 def scatter_kernel(
     back, pg, pu, pd,
     back_o, rg, ru, rd,
-    tmp, summed, back_send, back_recv, p_send, p_recv, local_sem,
+    tmp, summed, staged, back_send, back_recv, p_send, p_recv, fetch_sem, local_sem,
 ):
     rep, exp = lax.axis_index("rep"), lax.axis_index("exp")
     x_rep, y_rep, diag = rep_neighbours(rep)
@@ -217,7 +224,10 @@
     for k in range(3):
         for way in range(2):
             direct(k, way).start()
-    own = pltpu.make_async_copy(back.at[exp], back_o.at[exp], local_sem)
+    fetch = pltpu.make_async_copy(back.at[exp], staged, fetch_sem)
+    fetch.start()
+    fetch.wait()
+    own = pltpu.make_async_copy(staged, back_o.at[exp], local_sem)
     own.start()
     for k in range(3):
         for way in range(2):
@@ -270,9 +280,15 @@
         out_specs=(ANY,) * 6,
         scratch_shapes=[
             DMA((2, 4, 3)), DMA((2, 8)), DMA((7,)), DMA((8,)),
-            DMA((3, 2, 2)), DMA((3, 2)), DMA((3, 4, 2)), DMA((6,)),
+            DMA((3, 2, 2)), DMA((3, 2)), DMA((3, 4, 2)), DMA((6,)), DMA((6,)),
+        ]
+        + [
+            pltpu.VMEM(a.shape, a.dtype)
+            for a in (tokens, grad_out, info, w_gate, w_up, w_down)
         ],
-        compiler_params=pltpu.CompilerParams(collective_id=0, has_side_effects=True),
+        compiler_params=pltpu.CompilerParams(
+            collective_id=0, has_side_effects=True, vmem_limit_bytes=16 * 1024 * 1024
+        ),
     )(tokens, grad_out, info, w_gate, w_up, w_down)
 
 
@@ -287,7 +303,8 @@
         scratch_shapes=[
             pltpu.VMEM((3, 2, depth // 2, width), BF16),
             pltpu.VMEM((3, 2, depth // 2, width), BF16),
-            DMA((7,)), DMA((8,)), DMA((3, 2, 3)), DMA((3, 2, 3)), DMA,
+            pltpu.VMEM(back.shape[1:], BF16),
+            DMA((7,)), DMA((8,)), DMA((3, 2, 3)), DMA((3, 2, 3)), DMA, DMA,
         ],
         compiler_params=pltpu.CompilerParams(
             collective_id=1, has_side_effects=True, vmem_limit_bytes=32 * 1024 * 1024
@@ -361,9 +378,9 @@
         row_grad.reshape(expert_count, slot_cap, model_width), *terms
     )
     grads = [
-        contract_rows(lax.dynamic_slice_in_dim(a, rep * depth, depth, 1), b)
+        lax.dynamic_index_in_dim(term, rep, 0, keepdims=False).astype(F32)
         + got[0].astype(F32) + got[1].astype(F32)
-        for (a, b), got in zip(pairs, received)
+        for term, got in zip(terms, received)
     ]
     slots = slots_of(routes, expert_count, slot_cap).astype(BF16)
     grad_in = contract_rows(

time: 231 us -> 195 us (0.84)
  Pallas kernels: 191 us -> 164 us
  matrix products: 30 us -> 18.3 us
    pallas_call x1, Pallas kernels: 111 us -> 84.5 us  [gather_all(): pl.pallas_call(gather_kernel, out_shape=(rows, rows, jax.ShapeDtypeStruct...]
    dot_general x7 -> x4, matrix products: 16.4 us -> 7.15 us  [contract_rows(): lax.dot_general(left, right, (((0,), (0,)), ((), ())), preferred_element_...]
    add x0 -> x2, other arithmetic: none -> 3.57 us  [block_of_mesh(): lax.dynamic_index_in_dim(term, rep, 0, keepdims=False).astype(F32)]
    dot_general x1, matrix products: 3.04 us -> 0.7 us  [block_of_mesh(): into(pick, all_tok).astype(BF16)]
    unnamed x32 -> x10, local copies, waits for them, and re-layouts: 6.21 us -> 5.48 us
where the time goes in v2:
time: 195 us
  Pallas kernels  164 us (84%)
  matrix products  18.3 us (9%)
  local copies, waits for them, and re-layouts  6.32 us (3%)
  other arithmetic  5.18 us (3%)
    pallas_call x1, Pallas kernels, gather_all(): pl.pallas_call(gather_kernel, out_shape=(rows, rows, jax.ShapeDtypeStruct...  84.5 us
    pallas_call x1, Pallas kernels, scatter_all(): pl.pallas_call(scatter_kernel, out_shape=(jax.ShapeDtypeStruct(back.shape...  79.5 us
    dot_general x4, matrix products, contract_rows(): lax.dot_general(left, right, (((0,), (0,)), ((), ())), preferred_element_...  7.15 us
    unnamed x10, local copies, waits for them, and re-layouts  5.48 us

profile of v2, /device:TPU:0, one launch (start us, length us, event | category | flops | bytes accessed | tf_op | source)
XLA Modules:
  0.0 194.5 jit_solution(6335923541796036014)
XLA Ops:
  0.6 0.1 pad.2.clone
  0.7 0.7 convert_bitcast_fusion
  1.4 0.8 slice_bitcast_fusion.1
  2.2 0.7 maximum_maximum_fusion.info
  2.9 0.1 fusion.2
  3.0 0.0 copy-start
  3.0 1.1 copy-done
  4.2 0.0 copy-start.1
  4.2 1.1 copy-done.1
  5.3 0.0 copy-start.2
  5.3 1.1 copy-done.2
  6.4 0.0 copy-start.3
  6.5 1.0 copy-done.3
  7.5 0.0 copy-start.4
  7.5 1.0 copy-done.4
  8.5 84.5 %shard_map.102 = (bf16[8,128,2048]{2,1,0:T(8,128)(2,1)S(1)}, bf16[8,128,2048]{2,1,0:T(8,128)(2,1)S(1)}, f32[8,8,128]{2,1,0:T(8,128)S(1)}, bf16[4,512,768]{2,1,0:...) custom-call(bf16[128,2048]{1,0:T(8,128)(2,1)S(1)} %copy-done.3, ...), custom_call_target="tpu_custom_call" | custom-call | tf_op jit(solution)/shard_map/pallas_call | solution.py:276
  93.1 0.1 fusion.3
  93.2 0.7 convolution_convert_fusion.3
  93.9 0.1 select_reduce_fusion
  94.1 0.7 multiply_convert_fusion
  94.8 1.8 fusion.16
  96.6 1.8 fusion.15
  98.4 2.2 %multiply_convert_fusion.2 = (bf16[512,768]{1,0:T(8,128)(2,1)S(1)}, bf16[512,768]{1,0:T(8,128)(2,1)S(1)}) fusion(f32[512,768]{1,0:T(8,128)S(1)} %fusion.16, f32[512,768]{1,0:T(8,128)S(1)} %fusion.15, bf16[512,2048]{1,0:T(8,128)(2,1)S(1)} %bitcast.60, bf16[2048,768]{1,0:T(8,128)(2,1)S(1)} %bitcast.59), kind=kOutput, calls=%fused_computation.12 | convolution fusion | flops 1615724544 | bytes 9961472 | tf_op jit(solution)/shard_map/dot_general | solution.py:318
  100.6 2.0 %convolution_convert_fusion = bf16[2048,768]{1,0:T(8,128)(2,1)S(1)} fusion(bf16[512,2048]{1,0:T(8,128)(2,1)S(1)} %bitcast.61, f32[512,768]{1,0:T(8,128)S(1)} %fusion.15, f32[512,768]{1,0:T(8,128)S(1)} %fusion.16), kind=kOutput, calls=%fused_computation.2 | convolution fusion | flops 1614544896 | bytes 8388608 | tf_op jit(solution)/shard_map/dot_general | solution.py:16
  102.6 1.8 fusion.17
  104.4 1.8 add_convert_fusion
  106.2 2.0 %convolution_convert_fusion.1 = bf16[2048,768]{1,0:T(8,128)(2,1)S(1)} fusion(bf16[512,2048]{1,0:T(8,128)(2,1)S(1)} %bitcast.64, bf16[512,768]{1,0:T(8,128)(2,1)S(1)} %get-tuple-element.24), kind=kOutput, calls=%fused_computation.3 | convolution fusion | flops 1612185600 | bytes 6029312 | tf_op jit(solution)/shard_map/dot_general | solution.py:16
  108.3 1.8 convolution_convert_fusion.2
  110.1 79.5 %shard_map.103 = (bf16[8,64,2048]{2,1,0:T(8,128)(2,1)S(1)}, bf16[2,512,768]{2,1,0:T(8,128)(2,1)S(1)}, bf16[2,512,768]{2,1,0:T(8,128)(2,1)S(1)}, bf16[2,512,768]{2,1,0:T(8,128)(2,1)S(1)}) custom-call(bf16[8,64,2048]{2,1,0:T(8,128)(2,1)S(1)} %bitcast.51, bf16[4,512,768]{2,1,0:T(8,128)(2,1)S(1)} %bitcast.45, bf16[4,512,768]{2,1,0:T(8,128)(2,1)S(1)} %bitcast.49, ...), custom_call_target="tpu_custom_call" | custom-call | tf_op jit(solution)/shard_map/pallas_call | solution.py:298
  189.7 2.2 %convert_add_fusion = (f32[1,512,768]{2,1,0:T(8,128)}, f32[1,512,768]{2,1,0:T(8,128)}) fusion(bf16[2,512,768]{2,1,0:T(8,128)(2,1)S(1)} %get-tuple-element.22, bf16[4,512,768]{2,1,0:T(8,128)(2,1)S(1)} %bitcast.48, s32[]{:T(128)S(6)} %select_n.31, bf16[2,512,768]{2,1,0:T(8,128)(2,1)S(1)} %get-tuple-element.21, bf16[4,512,768]{2,1,0:T(8,128)(2,1)S(1)} %bitcast.50), kind=kLoop, calls=%fused_computation.8 | loop fusion | flops 3932160 | bytes 7864324 | tf_op jit(solution)/shard_map/add | solution.py:381
  191.8 1.4 convert_add_fusion.2
  193.2 1.3 fusion
  (3 shorter events, 0.0 us)
Async XLA Ops:
  3.0 1.1 copy-start
  4.2 1.1 copy-start.1
  5.3 1.1 copy-start.2
  6.4 1.0 copy-start.3
  7.5 1.0 copy-start.4
